TPU v7x, 256 devices: a whole 4x4x8 slice. The times are simulated.
256 devices in a mesh: blk: 16 (over y_hi, z), frames: 16 (over x, y_lo, core).
Axes of the slice: x: 4, y: 4 (y_hi: 2, y_lo: 2; y = y_hi * 2 + y_lo), z: 8, core: 2. Of those that a mesh axis runs over, the one named last changes fastest.
Arguments:
- coarse_query: bfloat16 [512, 16, 256], P('blk'), may hold values from -125 to 125
- coarse_feat: bfloat16 [64, 8160, 256], P('frames', 'blk'), may hold values from -61 to 61
- fine_query: bfloat16 [512, 128], P(('blk', 'frames')), may hold values from -175 to 175
- fine_tiles: bfloat16 [64, 1024, 64, 128], P('frames', 'blk'), may hold values from -61 to 61
- track_pos: int32 [2, 64, 512], P(None, None, ('blk', 'frames')), may hold values from 0 to 959, as said below
- tile_list: int32 [64, 16, 16, 8], P('frames', 'blk'), may hold values from 0 to 63, as said below
- tile_valid: int32 [64, 16, 16, 8], P('frames', 'blk'), may hold values from 0 to 1, as said below
Outputs:
- coarse_pos: float32 [2, 64, 512], P(None, 'frames', 'blk')
- fine_offset: float32 [2, 64, 512], P(None, None, ('blk', 'frames'))
Inputs may be any that keep to these rules, and one draw needn't show every extreme that they name: `tile_list`: in each list the valid slots come first and name distinct tiles of the group's window; padded slots hold 63; in every frame and group some owner's list is full. `tile_valid`: each list has at least 4 valid slots. `track_pos`: rows lie below 544 and columns below 960.
All inputs are finite; a program needn't handle non-finite values.
Results may differ from a plain program's by a relative error of at most 0.0003.
Values may be sent and summed in bfloat16 or wider, within the bound.
A program may use at most 192 MiB of HBM per device.

v0:
```python
import math
import jax
import jax.numpy as jnp
from jax import lax
from jax.sharding import PartitionSpec as P

GH = 68
GW = 120
TILE = 8
SPREAD = 32.0


def coarse(coarse_query, coarse_feat):
    track_group, heads, channels = coarse_query.shape
    frames_here, region, _ = coarse_feat.shape
    blocks = lax.axis_size("blk")
    scale = 1.0 / math.sqrt(channels)
    start = lax.axis_index("blk") * region
    queries = lax.all_gather(coarse_query.reshape(track_group * heads, channels), "blk", axis=0)
    positions = start + jnp.arange(region, dtype=jnp.int32)
    pos_row = (positions // GW).astype(jnp.float32)
    pos_col = (positions % GW).astype(jnp.float32)
    scores = (
        jnp.einsum("brc,fpc->bfpr", queries, coarse_feat, preferred_element_type=jnp.float32)
        * scale
    )
    top = jnp.max(scores, axis=2)
    weights = jnp.exp(scores - top[:, :, None])
    stats = jnp.stack(
        [
            top,
            jnp.sum(weights, axis=2),
            jnp.sum(weights * pos_row[None, None, :, None], axis=2),
            jnp.sum(weights * pos_col[None, None, :, None], axis=2),
        ],
        axis=1,
    )
    stats = lax.all_to_all(stats, "blk", split_axis=0, concat_axis=0, tiled=True)
    top = jnp.max(stats[:, 0], axis=0, keepdims=True)
    factor = jnp.exp(stats[:, 0] - top)
    total = jnp.sum(stats[:, 1] * factor, axis=0)
    rows = jnp.sum(stats[:, 2] * factor, axis=0) / total
    cols = jnp.sum(stats[:, 3] * factor, axis=0) / total
    rows = jnp.mean(rows.reshape(frames_here, track_group, heads), axis=2)
    cols = jnp.mean(cols.reshape(frames_here, track_group, heads), axis=2)
    return jnp.stack([(rows - (GH - 1) / 2.0) / (GH / 4.0), (cols - (GW - 1) / 2.0) / (GW / 4.0)])


def fine(fine_query, fine_tiles, track_pos, tile_list, tile_valid, region):
    frames_here, tiles, cells, channels = fine_tiles.shape
    owners = tile_list.shape[2]
    owned = fine_query.shape[0]
    start = lax.axis_index("blk") * region
    descs = lax.all_gather(fine_query, "frames", axis=0, tiled=True)
    places = lax.all_to_all(track_pos, "frames", split_axis=1, concat_axis=2, tiled=True).astype(
        jnp.float32
    )
    scores = jnp.einsum(
        "nc,fkc->fnk",
        descs,
        fine_tiles.reshape(frames_here, tiles * cells, channels),
        preferred_element_type=jnp.float32,
    ) * (1.0 / math.sqrt(channels))
    ids = tile_list[:, 0]
    live = tile_valid[:, 0]
    listed = jnp.any((ids[:, :, :, None] == jnp.arange(tiles)) & (live[:, :, :, None] > 0), axis=2)
    listed = jnp.repeat(jnp.repeat(listed, owned, axis=1), cells, axis=2)
    index = jnp.arange(tiles * cells, dtype=jnp.int32)
    cell = start + index // cells
    inner = index % cells
    row = (cell // GW * TILE + inner // TILE).astype(jnp.float32)
    col = (cell % GW * TILE + inner % TILE).astype(jnp.float32)
    away_row = row - places[0][:, :, None]
    away_col = col - places[1][:, :, None]
    scores = scores - (away_row**2 + away_col**2) * (0.5 / (SPREAD * SPREAD))
    scores = jnp.where(listed, scores, -1e30)
    weights = jnp.exp(scores - jnp.max(scores, axis=2, keepdims=True))
    total = jnp.sum(weights, axis=2)
    out = jnp.stack(
        [
            jnp.sum(weights * away_row, axis=2) / total / SPREAD,
            jnp.sum(weights * away_col, axis=2) / total / SPREAD,
        ]
    )
    return lax.all_to_all(out, "frames", split_axis=2, concat_axis=1, tiled=True)


def body(coarse_query, coarse_feat, fine_query, fine_tiles, track_pos, tile_list, tile_valid):
    offset = fine(fine_query, fine_tiles, track_pos, tile_list, tile_valid, coarse_feat.shape[1])
    return (coarse(coarse_query, coarse_feat), offset)


def solution(mesh):
    return jax.shard_map(
        body,
        mesh=mesh,
        in_specs=(
            P("blk", None, None),
            P("frames", "blk", None),
            P(("blk", "frames"), None),
            P("frames", "blk", None, None),
            P(None, None, ("blk", "frames")),
            P("frames", "blk", None, None),
            P("frames", "blk", None, None),
        ),
        out_specs=(P(None, "frames", "blk"), P(None, None, ("blk", "frames"))),
        check_vma=False,
    )
```

profile of v0, /device:TPU:2, one launch (start us, length us, event | category | flops | bytes accessed | tf_op | source)
XLA Modules:
  0.0 203.0 jit_solution(1856049340781756826)
XLA Ops:
  7.2 0.0 all-gather.3.cloned.1.call-start
  7.2 0.7 all-gather.3.cloned.1.call-update
  7.9 1.4 copy.87
  9.3 5.9 %all-to-all-start.1 = ((s32[2,64,2]{2,0,1:T(2,128)}), s32[2,64,2]{2,0,1:T(2,128)S(1)}, u32[]{:S(2)}, u32[]{:S(2)}) async-start(s32[2,64,2]{2,0,1:T(2,128)} %copy.87), calls=%async_computation.1 | async-start | bytes 131072 | tf_op jit(solution)/shard_map/all_to_all | solution.py:55
  15.2 0.8 copy.83
  16.0 0.7 compare_bitcast_fusion
  16.7 0.1 copy.84
  16.8 0.2 fusion.16
  17.1 17.5 %all-gather = bf16[16,2,128]{2,1,0:T(2,128)(2,1)S(1)} all-gather(bf16[1,2,128]{2,1,0:T(2,128)(2,1)} %bitcast.111), channel_id=1, replica_groups=mesh['blk'=16,'frames'=16] {'frames'}, dimensions={0}, use_global_device_ids=true | all-gather | bytes 8704 | tf_op jit(solution)/shard_map/all_gather | solution.py:54
  34.6 1.4 broadcast_in_dim.9
  36.0 2.6 %reshape.202 = pred[4,32,4096]{2,1,0:T(32,128)(4,1)S(1)} reshape(pred[4,32,64,64]{3,2,1,0:T(32,128)(4,1)S(1)} %broadcast_in_dim.9) | data formatting | bytes 1048576 | tf_op jit(solution)/shard_map/reshape | solution.py:67
  38.6 0.0 all-to-all-done.1
  38.6 0.1 copy.88
  38.7 0.1 convert_element_type.42
  38.8 0.1 copy.90
  38.9 0.1 copy.92
  39.0 0.0 copy-start
  39.0 4.6 %fusion.12 = (f32[4,32]{1,0:T(4,128)S(1)}, f32[4,32]{1,0:T(4,128)S(1)}, f32[4,32]{1,0:T(4,128)S(1)}) fusion(f32[4,32]{1,0:T(4,128)S(1)} %copy.90, f32[4096]{0:T(1024)S(1)} %get-tuple-element.19, f32[4,32]{1,0:T(4,128)S(1)} %copy.92, f32[4096]{0:T(1024)S(1)} %get-tuple-element.20, pred[4,32,4096]{2,1,0:T(32,128)(4,1)S(1)} %reshape.202, ...), kind=kOutput, calls=%fused_computation.21 | convolution fusion | flops 143134464 | bytes 4762112 | tf_op jit(solution)/shard_map/sub | solution.py:77
  43.6 0.7 copy.93
  44.3 6.0 %all-to-all-start.2 = ((f32[2,4,32]{1,0,2:T(2,128)}), f32[2,4,32]{1,0,2:T(2,128)S(1)}, u32[]{:S(2)}, u32[]{:S(2)}) async-start(f32[2,4,32]{1,0,2:T(2,128)} %copy.93), calls=%async_computation.2 | async-start | bytes 65536 | tf_op jit(solution)/shard_map/all_to_all | solution.py:85
  50.3 63.3 %all-gather.3.cloned.1.call-done = bf16[16,512,256]{2,1,0:T(8,128)(2,1)} async-done(((bf16[1,512,256]{2,1,0:T(8,128)(2,1)}), bf16[16,512,256]{2,1,0:T(8,128)(2,1)}) %all-gather.3.cloned.1.call-update) | async-done | bytes 4194320 | tf_op jit(solution)/shard_map/all_gather | solution.py:19
  113.6 0.0 copy-done
  113.6 25.3 %bitcast_reduce_fusion = (f32[16,4,512]{2,0,1:T(8,128)S(1)}, f32[4,510,16,512]{3,1,2,0:T(8,128)}) fusion(bf16[16,512,256]{2,1,0:T(8,128)(2,1)} %all-gather.3.cloned.1.call-done, bf16[4,510,256,1]{2,0,1,3:T(4,128)(2,1)S(1)} %bitcast.99), kind=kOutput, calls=%fused_computation.2 | convolution fusion | flops 8589770752 | bytes 72216576 | tf_op jit(solution)/shard_map/brc,fpc->bfpr/dot_general | solution.py:24
  138.9 36.5 %fusion.2 = (f32[16,4,512]{2,0,1:T(8,128)S(1)}, f32[16,4,512]{2,0,1:T(8,128)S(1)}, f32[16,4,512]{2,0,1:T(8,128)S(1)}) fusion(f32[4,510,16,512]{3,1,2,0:T(8,128)} %get-tuple-element.18, f32[16,4,512]{2,0,1:T(8,128)S(1)} %get-tuple-element.17, f32[510]{0:T(512)S(1)} %get-tuple-element.22, f32[510]{0:T(512)S(1)} %get-tuple-element.21), kind=kLoop, calls=%fused_computation.6 | loop fusion | flops 116883456 | bytes 67375088 | tf_op jit(solution)/shard_map/reduce_sum | solution.py:32
  175.5 1.1 copy.79
  176.7 0.0 all-to-all-done.2
  176.7 4.2 %all-to-all-start = ((f32[16,4,4,512]{3,2,1,0:T(4,128)}), f32[16,4,4,512]{3,2,1,0:T(4,128)S(1)}, u32[]{:S(2)}, u32[]{:S(2)}) async-start(f32[16,4,4,512]{3,2,1,0:T(4,128)} %copy.79), calls=%async_computation | async-start | bytes 1048576 | tf_op jit(solution)/shard_map/all_to_all | solution.py:38
  180.9 0.7 all_to_all.28
  181.5 13.4 %all-to-all-done = f32[16,4,4,512]{3,2,1,0:T(4,128)S(1)} async-done(((f32[16,4,4,512]{3,2,1,0:T(4,128)}), f32[16,4,4,512]{3,2,1,0:T(4,128)S(1)}, u32[]{:S(2)}, u32[]{:S(2)}) %all-to-all-start) | async-done | bytes 524320 | tf_op jit(solution)/shard_map/all_to_all | solution.py:38
  195.0 0.1 fusion.22
  195.1 0.1 div.112
  195.2 0.1 reduce_sum.106
  195.3 0.1 div.106
  195.4 0.1 reduce_sum.104
  195.5 0.6 pad_maximum_fusion.1
  (18 shorter events, 0.2 us)
Async XLA Ops:
  7.2 106.4 %all-gather.3.cloned.1.call-start = ((), (), s32[]{:S(2)}) async-start(), calls=%async_computation.3 | async-start | bytes 4456448 | tf_op jit(solution)/shard_map/all_gather | solution.py:19
  9.3 29.3 %all-to-all-start.1 = ((s32[2,64,2]{2,0,1:T(2,128)}), s32[2,64,2]{2,0,1:T(2,128)S(1)}, u32[]{:S(2)}, u32[]{:S(2)}) async-start(s32[2,64,2]{2,0,1:T(2,128)} %copy.87), calls=%async_computation.1 | async-start | bytes 131072 | tf_op jit(solution)/shard_map/all_to_all | solution.py:55
  39.0 74.6 %copy-start = (bf16[4,510,256]{2,0,1:T(4,128)(2,1)S(1)}, bf16[4,510,256]{2,0,1:T(4,128)(2,1)}, u32[]{:S(2)}) copy-start(bf16[4,510,256]{2,0,1:T(4,128)(2,1)} %param.8) | copy-start | bytes 3133444
  44.3 132.3 %all-to-all-start.2 = ((f32[2,4,32]{1,0,2:T(2,128)}), f32[2,4,32]{1,0,2:T(2,128)S(1)}, u32[]{:S(2)}, u32[]{:S(2)}) async-start(f32[2,4,32]{1,0,2:T(2,128)} %copy.93), calls=%async_computation.2 | async-start | bytes 65536 | tf_op jit(solution)/shard_map/all_to_all | solution.py:85
  176.7 18.3 %all-to-all-start = ((f32[16,4,4,512]{3,2,1,0:T(4,128)}), f32[16,4,4,512]{3,2,1,0:T(4,128)S(1)}, u32[]{:S(2)}, u32[]{:S(2)}) async-start(f32[16,4,4,512]{3,2,1,0:T(4,128)} %copy.79), calls=%async_computation | async-start | bytes 1048576 | tf_op jit(solution)/shard_map/all_to_all | solution.py:38
Sparse Core Ops, SparseCore 0:
  10.6 102.9 all-gather.2
where the time goes:
time: 203 us
  waiting for transfers between devices  77.4 us (38%)
  other arithmetic  38.6 us (19%)
  matrix products  29.9 us (15%)
  blocking collectives  17.5 us (9%)
  starting transfers between devices  16.1 us (8%)
  between operations  14.2 us (7%)
  local copies, waits for them, and re-layouts  9.39 us (5%)
    all_gather x1, waiting for transfers between devices, coarse(): lax.all_gather(coarse_query.reshape(track_group * heads, channels), 'blk'...  63.3 us
    reduce_sum x1, other arithmetic, coarse(): jnp.sum(weights, axis=2)  36.5 us
    dot_general x1, matrix products, coarse(): jnp.einsum('brc,fpc->bfpr', queries, coarse_feat, preferred_element_type=...  25.3 us
    all_gather x1, blocking collectives, fine(): descs = lax.all_gather(fine_query, 'frames', axis=0, tiled=True)  17.5 us
    all_to_all x1, waiting for transfers between devices, coarse(): lax.all_to_all(stats, 'blk', split_axis=0, concat_axis=0, tiled=True)  13.4 us
    all_to_all x1, starting transfers between devices, fine(): lax.all_to_all(out, 'frames', split_axis=2, concat_axis=1, tiled=True)  5.99 us
    all_to_all x1, starting transfers between devices, fine(): lax.all_to_all(track_pos, 'frames', split_axis=1, concat_axis=2, tiled=True)  5.86 us
    sub x1, matrix products, fine(): weights = jnp.exp(scores - jnp.max(scores, axis=2, keepdims=True))  4.61 us
  transfers between devices with their start and end apart: 4, of which 2 were waited for; matrix products, arithmetic and copies ran while one was open for 37% of the time, Pallas kernels for 0%

commit v1 on v0

--- a/solution.py
+++ b/solution.py
@@ -51,7 +51,10 @@
     owners = tile_list.shape[2]
     owned = fine_query.shape[0]
     start = lax.axis_index("blk") * region
-    descs = lax.all_gather(fine_query, "frames", axis=0, tiled=True)
+    pages = []
+    for _ in range(jax.lax.psum(1, "frames")):
+        pages.append(fine_query)
+    descs = jnp.concatenate(jax.lax.all_to_all(jnp.stack(pages), "frames", 0, 0), 0)
     places = lax.all_to_all(track_pos, "frames", split_axis=1, concat_axis=2, tiled=True).astype(
         jnp.float32
     )

time: 203 us -> 204 us (level)
  blocking collectives: 17.5 us -> 0 us
  waiting for transfers between devices: 77.4 us -> 89.6 us
  starting transfers between devices: 16.1 us -> 20.5 us
    all_gather x1 -> x0, blocking collectives: 17.5 us -> none  [fine(): descs = lax.all_gather(fine_query, 'frames', axis=0, tiled=True)]
    all_gather x1, waiting for transfers between devices: 63.3 us -> 71.2 us  [coarse(): lax.all_gather(coarse_query.reshape(track_group * heads, channels), 'blk'...]
    all_to_all x0 -> x1, starting transfers between devices: none -> 5.72 us  [fine(): jax.lax.all_to_all(jnp.stack(pages), 'frames', 0, 0)]
    all_to_all x0 -> x1, waiting for transfers between devices: none -> 4.29 us  [fine(): jax.lax.all_to_all(jnp.stack(pages), 'frames', 0, 0)]
  transfers between devices with their start and end apart: 4 -> 5, of which waited for: 2 -> 3; matrix products, arithmetic and copies ran while one was open for 37% -> 38% of each run, Pallas kernels for 0% -> 0%
where the time goes in v1:
time: 204 us; the launch traced here: 203 us
  waiting for transfers between devices  89.6 us (44%)
  other arithmetic  38.6 us (19%)
  matrix products  30 us (15%)
  starting transfers between devices  20.5 us (10%)
  between operations  14.2 us (7%)
  local copies, waits for them, and re-layouts  10 us (5%)
    all_gather x1, waiting for transfers between devices, coarse(): lax.all_gather(coarse_query.reshape(track_group * heads, channels), 'blk'...  71.2 us
    reduce_sum x1, other arithmetic, coarse(): jnp.sum(weights, axis=2)  36.5 us
    dot_general x1, matrix products, coarse(): jnp.einsum('brc,fpc->bfpr', queries, coarse_feat, preferred_element_type=...  25.3 us
    all_to_all x1, waiting for transfers between devices, coarse(): lax.all_to_all(stats, 'blk', split_axis=0, concat_axis=0, tiled=True)  13.4 us
    all_to_all x1, starting transfers between devices, fine(): lax.all_to_all(track_pos, 'frames', split_axis=1, concat_axis=2, tiled=True)  5.86 us
    all_to_all x1, starting transfers between devices, fine(): jax.lax.all_to_all(jnp.stack(pages), 'frames', 0, 0)  5.72 us
    all_to_all x1, starting transfers between devices, fine(): lax.all_to_all(out, 'frames', split_axis=2, concat_axis=1, tiled=True)  4.74 us
    sub x1, matrix products, fine(): weights = jnp.exp(scores - jnp.max(scores, axis=2, keepdims=True))  4.66 us
  transfers between devices with their start and end apart: 5, of which 3 were waited for; matrix products, arithmetic and copies ran while one was open for 38% of the time, Pallas kernels for 0%

profile of v1, /device:TPU:2, one launch (start us, length us, event | category | flops | bytes accessed | tf_op | source)
XLA Modules:
  0.0 203.0 jit_solution(5525858089319309331)
XLA Ops:
  7.2 0.0 copy-start.1
  7.2 0.0 all-gather.2.cloned.1.call-start
  7.2 0.7 all-gather.2.cloned.1.call-update
  7.9 1.4 copy.87
  9.3 5.9 %all-to-all-start.2 = ((s32[2,64,2]{2,0,1:T(2,128)}), s32[2,64,2]{2,0,1:T(2,128)S(1)}, u32[]{:S(2)}, u32[]{:S(2)}) async-start(s32[2,64,2]{2,0,1:T(2,128)} %copy.87), calls=%async_computation.2 | async-start | bytes 131072 | tf_op jit(solution)/shard_map/all_to_all | solution.py:58
  15.2 0.8 copy.83
  16.0 0.7 compare_bitcast_fusion
  16.7 0.1 copy.84
  16.8 0.2 fusion.16
  17.1 1.4 broadcast_in_dim.9
  18.5 2.7 %reshape.207 = pred[4,32,4096]{2,1,0:T(32,128)(4,1)S(1)} reshape(pred[4,32,64,64]{3,2,1,0:T(32,128)(4,1)S(1)} %broadcast_in_dim.9) | data formatting | bytes 1048576 | tf_op jit(solution)/shard_map/reshape | solution.py:70
  21.2 0.0 all-to-all-done.2
  21.2 0.0 copy-done.1
  21.2 0.6 stack.22
  21.8 5.7 %all-to-all-start.1 = ((bf16[16,2,128]{2,1,0:T(2,128)(2,1)}), bf16[16,2,128]{2,1,0:T(2,128)(2,1)S(1)}, u32[]{:S(2)}, u32[]{:S(2)}) async-start(bf16[16,2,128]{2,1,0:T(2,128)(2,1)} %stack.22), calls=%async_computation.1 | async-start | bytes 16384 | tf_op jit(solution)/shard_map/all_to_all | solution.py:57
  27.5 0.1 copy.88
  27.6 0.1 convert_element_type.42
  27.8 0.1 copy.90
  27.9 0.1 copy.92
  27.9 4.3 %all-to-all-done.1 = bf16[16,2,128]{2,1,0:T(2,128)(2,1)S(1)} async-done(((bf16[16,2,128]{2,1,0:T(2,128)(2,1)}), bf16[16,2,128]{2,1,0:T(2,128)(2,1)S(1)}, u32[]{:S(2)}, u32[]{:S(2)}) %all-to-all-start.1) | async-done | bytes 8224 | tf_op jit(solution)/shard_map/all_to_all | solution.py:57
  32.2 0.0 copy-start
  32.2 4.7 %fusion.12 = (f32[4,32]{1,0:T(4,128)S(1)}, f32[4,32]{1,0:T(4,128)S(1)}, f32[4,32]{1,0:T(4,128)S(1)}) fusion(f32[4,32]{1,0:T(4,128)S(1)} %copy.90, f32[4096]{0:T(1024)S(1)} %get-tuple-element.19, f32[4,32]{1,0:T(4,128)S(1)} %copy.92, f32[4096]{0:T(1024)S(1)} %get-tuple-element.20, pred[4,32,4096]{2,1,0:T(32,128)(4,1)S(1)} %reshape.207, ...), kind=kOutput, calls=%fused_computation.21 | convolution fusion | flops 143134464 | bytes 4762112 | tf_op jit(solution)/shard_map/sub | solution.py:80
  36.9 0.7 copy.93
  37.6 4.7 %all-to-all-start.3 = ((f32[2,4,32]{1,0,2:T(2,128)}), f32[2,4,32]{1,0,2:T(2,128)S(1)}, u32[]{:S(2)}, u32[]{:S(2)}) async-start(f32[2,4,32]{1,0,2:T(2,128)} %copy.93), calls=%async_computation.3 | async-start | bytes 65536 | tf_op jit(solution)/shard_map/all_to_all | solution.py:88
  42.4 71.2 %all-gather.2.cloned.1.call-done = bf16[16,512,256]{2,1,0:T(8,128)(2,1)} async-done(((bf16[1,512,256]{2,1,0:T(8,128)(2,1)}), bf16[16,512,256]{2,1,0:T(8,128)(2,1)}) %all-gather.2.cloned.1.call-update) | async-done | bytes 4194320 | tf_op jit(solution)/shard_map/all_gather | solution.py:19
  113.6 0.0 copy-done
  113.6 25.3 %bitcast_reduce_fusion = (f32[16,4,512]{2,0,1:T(8,128)S(1)}, f32[4,510,16,512]{3,1,2,0:T(8,128)}) fusion(bf16[16,512,256]{2,1,0:T(8,128)(2,1)} %all-gather.2.cloned.1.call-done, bf16[4,510,256,1]{2,0,1,3:T(4,128)(2,1)S(1)} %bitcast.98), kind=kOutput, calls=%fused_computation.2 | convolution fusion | flops 8589770752 | bytes 72216576 | tf_op jit(solution)/shard_map/brc,fpc->bfpr/dot_general | solution.py:24
  138.9 36.5 %fusion.2 = (f32[16,4,512]{2,0,1:T(8,128)S(1)}, f32[16,4,512]{2,0,1:T(8,128)S(1)}, f32[16,4,512]{2,0,1:T(8,128)S(1)}) fusion(f32[4,510,16,512]{3,1,2,0:T(8,128)} %get-tuple-element.18, f32[16,4,512]{2,0,1:T(8,128)S(1)} %get-tuple-element.17, f32[510]{0:T(512)S(1)} %get-tuple-element.22, f32[510]{0:T(512)S(1)} %get-tuple-element.21), kind=kLoop, calls=%fused_computation.6 | loop fusion | flops 116883456 | bytes 67375088 | tf_op jit(solution)/shard_map/reduce_sum | solution.py:32
  175.5 1.1 copy.79
  176.7 0.0 all-to-all-done.3
  176.7 4.2 %all-to-all-start = ((f32[16,4,4,512]{3,2,1,0:T(4,128)}), f32[16,4,4,512]{3,2,1,0:T(4,128)S(1)}, u32[]{:S(2)}, u32[]{:S(2)}) async-start(f32[16,4,4,512]{3,2,1,0:T(4,128)} %copy.79), calls=%async_computation | async-start | bytes 1048576 | tf_op jit(solution)/shard_map/all_to_all | solution.py:38
  180.9 0.7 all_to_all.32
  181.5 13.4 %all-to-all-done = f32[16,4,4,512]{3,2,1,0:T(4,128)S(1)} async-done(((f32[16,4,4,512]{3,2,1,0:T(4,128)}), f32[16,4,4,512]{3,2,1,0:T(4,128)S(1)}, u32[]{:S(2)}, u32[]{:S(2)}) %all-to-all-start) | async-done | bytes 524320 | tf_op jit(solution)/shard_map/all_to_all | solution.py:38
  195.0 0.1 fusion.22
  195.1 0.1 div.112
  195.2 0.1 reduce_sum.106
  195.3 0.1 div.106
  195.4 0.1 reduce_sum.104
  195.5 0.6 pad_maximum_fusion.1
  (18 shorter events, 0.2 us)
Async XLA Ops:
  7.2 14.1 %copy-start.1 = (bf16[2,128]{1,0:T(2,128)(2,1)S(1)}, bf16[2,128]{1,0:T(2,128)(2,1)}, u32[]{:S(2)}) copy-start(bf16[2,128]{1,0:T(2,128)(2,1)} %param.9) | copy-start | bytes 1540
  7.2 106.4 %all-gather.2.cloned.1.call-start = ((), (), s32[]{:S(2)}) async-start(), calls=%async_computation.4 | async-start | bytes 4456448 | tf_op jit(solution)/shard_map/all_gather | solution.py:19
  9.3 11.9 %all-to-all-start.2 = ((s32[2,64,2]{2,0,1:T(2,128)}), s32[2,64,2]{2,0,1:T(2,128)S(1)}, u32[]{:S(2)}, u32[]{:S(2)}) async-start(s32[2,64,2]{2,0,1:T(2,128)} %copy.87), calls=%async_computation.2 | async-start | bytes 131072 | tf_op jit(solution)/shard_map/all_to_all | solution.py:58
  21.8 10.4 %all-to-all-start.1 = ((bf16[16,2,128]{2,1,0:T(2,128)(2,1)}), bf16[16,2,128]{2,1,0:T(2,128)(2,1)S(1)}, u32[]{:S(2)}, u32[]{:S(2)}) async-start(bf16[16,2,128]{2,1,0:T(2,128)(2,1)} %stack.22), calls=%async_computation.1 | async-start | bytes 16384 | tf_op jit(solution)/shard_map/all_to_all | solution.py:57
  32.2 81.4 %copy-start = (bf16[4,510,256]{2,0,1:T(4,128)(2,1)S(1)}, bf16[4,510,256]{2,0,1:T(4,128)(2,1)}, u32[]{:S(2)}) copy-start(bf16[4,510,256]{2,0,1:T(4,128)(2,1)} %param.8) | copy-start | bytes 3133444
  37.6 139.0 %all-to-all-start.3 = ((f32[2,4,32]{1,0,2:T(2,128)}), f32[2,4,32]{1,0,2:T(2,128)S(1)}, u32[]{:S(2)}, u32[]{:S(2)}) async-start(f32[2,4,32]{1,0,2:T(2,128)} %copy.93), calls=%async_computation.3 | async-start | bytes 65536 | tf_op jit(solution)/shard_map/all_to_all | solution.py:88
  176.7 18.3 %all-to-all-start = ((f32[16,4,4,512]{3,2,1,0:T(4,128)}), f32[16,4,4,512]{3,2,1,0:T(4,128)S(1)}, u32[]{:S(2)}, u32[]{:S(2)}) async-start(f32[16,4,4,512]{3,2,1,0:T(4,128)} %copy.79), calls=%async_computation | async-start | bytes 1048576 | tf_op jit(solution)/shard_map/all_to_all | solution.py:38
Sparse Core Ops, SparseCore 0:
  10.6 102.9 all-gather.1
